TPU v7x, 128 devices: a whole 4x4x4 slice. The times are simulated.
128 devices in a mesh: seq: 16 (over x_lo, y, core), head: 8 (over z, x_hi).
Axes of the slice: x: 4 (x_hi: 2, x_lo: 2; x = x_hi * 2 + x_lo), y: 4, z: 4, core: 2. Of those that a mesh axis runs over, the one named last changes fastest.
Arguments:
- out_grad: bfloat16 [16384, 6144], P(('seq', 'head')), may hold values from -96 to 96
- expert_rows: bfloat16 [8, 8192, 6144], P('head', 'seq'), may hold values from -96 to 96
- expert_ids: int32 [16384, 2], P(('seq', 'head')), may hold values from 0 to 7, all different within a row; in each aligned block of 128 rows (0 to 127, 128 to 255, ...) at most 64 rows name the same one
- gates: float32 [16384, 2], P(('seq', 'head')), may hold values from 0.1 to 0.9
- out_proj: bfloat16 [3072, 6144], P('head'), may hold values from -0.078125 to 0.078125
- attention_output: bfloat16 [24, 16384, 128], P('head', 'seq'), may hold values from -0.0029296875 to 0.0029296875
- saved_queries: bfloat16 [24, 16384, 128], P('head', 'seq'), may hold values from -1.6953125 to 1.6953125
- saved_keys: bfloat16 [8, 16384, 128], P('head', 'seq'), may hold values from -1.6953125 to 1.6953125
- saved_values: bfloat16 [8, 16384, 128], P('head', 'seq'), may hold values from -6 to 6
- softmax_normalizer: float32 [24, 16384], P('head', 'seq'), may hold values from 8 to 9.5
Outputs:
- grad_query: bfloat16 [16384, 3072], P(('seq', 'head'))
- key_gradient_rows: bfloat16 [16384, 1024], P(('seq', 'head'))
- value_gradient_rows: bfloat16 [16384, 1024], P(('seq', 'head'))
- grad_proj: bfloat16 [3072, 6144], P('head')
Inputs may be any that keep to these rules, and one draw needn't show every extreme that they name: `expert_ids`: each row names 2 different experts. In each aligned block of 128 rows (the tokens of one device) no expert is named more than 64 times, a bound that some block reaches.
All inputs are finite; a program needn't handle non-finite values.
Results may differ from a plain program's by a relative error of at most 0.0065.
Values may be sent and summed in bfloat16 or wider, within the bound.
A program may use at most 128 MiB of HBM per device.

v0:
```python
import math
import jax
import jax.numpy as jnp
from jax import lax
from jax.sharding import PartitionSpec as P

WIN = 4096


def shifted(block, axis, distance):
    devices = range(lax.axis_size(axis))
    route = [(i - distance, i) for i in devices if i - distance in devices]
    return lax.ppermute(block, axis, route)


def routed_rows(returned, expert_ids):
    experts = returned.shape[0]
    capacity = returned.shape[1]
    model_width = returned.shape[2]
    pair_ids = expert_ids.reshape(-1)
    onehot = (pair_ids[:, None] == jnp.arange(experts, dtype=jnp.int32)[None, :]).astype(jnp.int32)
    before = jnp.cumsum(onehot, axis=0) - onehot
    slot_rank = jnp.sum(before * onehot, axis=1)
    flat_index = pair_ids * capacity + slot_rank
    row_table = returned.reshape(experts * capacity, model_width)
    picked = jnp.take(row_table, flat_index, axis=0)
    return picked.reshape(expert_ids.shape[0], expert_ids.shape[1], model_width)


def local(
    out_grad,
    expert_rows,
    expert_ids,
    gates,
    out_proj,
    attention_output,
    saved_queries,
    saved_keys,
    saved_values,
    softmax_normalizer,
):
    heads_dev, seq_dev, head_dim = saved_queries.shape
    kv_dev = saved_keys.shape[0]
    group_size = heads_dev // kv_dev
    model_width = out_grad.shape[1]
    returned = lax.all_to_all(expert_rows, "head", split_axis=1, concat_axis=0, tiled=True)
    picked = routed_rows(returned, expert_ids)
    summed = out_grad.astype(jnp.float32)
    summed = summed + gates[:, 0:1] * picked[:, 0].astype(jnp.float32)
    summed = summed + gates[:, 1:2] * picked[:, 1].astype(jnp.float32)
    hidden = summed.astype(jnp.bfloat16)
    piece = lax.all_gather(hidden, "head", axis=0, tiled=True)
    fresh_rows = lax.dot_general(
        piece, out_proj, (((1,), (1,)), ((), ())), preferred_element_type=jnp.float32
    ).astype(jnp.bfloat16)
    partial_value = lax.dot_general(
        attention_output, piece, (((1,), (0,)), ((), ())), preferred_element_type=jnp.float32
    )
    grad_out, partial_value = (fresh_rows, partial_value)
    summed_proj = lax.psum(partial_value, "seq")
    grad_proj = summed_proj.astype(jnp.bfloat16).reshape(heads_dev * head_dim, model_width)
    head_gradients = jnp.transpose(grad_out.reshape(seq_dev, heads_dev, head_dim), (1, 0, 2))
    row_delta = jnp.sum(
        head_gradients.astype(jnp.float32) * attention_output.astype(jnp.float32), axis=2
    )
    window = WIN
    span_count = (window + seq_dev - 1) // seq_dev
    offset = span_count * seq_dev
    kv_pair = jnp.stack([saved_keys, saved_values], axis=0)
    earlier = []
    for distance in range(span_count, 0, -1):
        earlier.append(shifted(kv_pair, "seq", distance))
    extended = jnp.concatenate(earlier + [kv_pair], axis=2)
    block_rows = min(512, seq_dev)
    key_span = window + block_rows
    score_scale = 1.0 / math.sqrt(head_dim)
    seq_pos = lax.axis_index("seq")
    rows_iota = lax.broadcasted_iota(jnp.int32, (block_rows, key_span), 0)
    cols_iota = lax.broadcasted_iota(jnp.int32, (block_rows, key_span), 1)
    in_band = (cols_iota >= rows_iota + 1) & (cols_iota <= rows_iota + window)
    ext_len = offset + seq_dev

    def block_step(index, carry):
        dk_ext, dv_ext, dq_all = carry
        first_row = index * block_rows
        key_start = first_row + (offset - window)
        usable = in_band & (cols_iota + key_start >= offset - seq_pos * seq_dev)
        key_blk = lax.dynamic_slice_in_dim(extended[0, 0], key_start, key_span, 0)
        value_blk = lax.dynamic_slice_in_dim(extended[1, 0], key_start, key_span, 0)
        dk_blk = jnp.zeros((key_span, head_dim), jnp.float32)
        dv_blk = jnp.zeros((key_span, head_dim), jnp.float32)
        for q_head in range(0, group_size):
            query_blk = lax.dynamic_slice_in_dim(saved_queries[q_head], first_row, block_rows, 0)
            grad_blk = lax.dynamic_slice(
                grad_out, (first_row, q_head * head_dim), (block_rows, head_dim)
            )
            lse_blk = lax.dynamic_slice_in_dim(softmax_normalizer[q_head], first_row, block_rows, 0)
            delta_blk = lax.dynamic_slice_in_dim(row_delta[q_head], first_row, block_rows, 0)
            scores = (
                lax.dot_general(
                    query_blk, key_blk, (((1,), (1,)), ((), ())), preferred_element_type=jnp.float32
                )
                * score_scale
            )
            probability = jnp.where(usable, jnp.exp(scores - lse_blk[:, None]), 0.0)
            grad_prob = lax.dot_general(
                grad_blk, value_blk, (((1,), (1,)), ((), ())), preferred_element_type=jnp.float32
            )
            grad_score = probability * (grad_prob - delta_blk[:, None])
            prob_half = probability.astype(jnp.bfloat16)
            score_half = grad_score.astype(jnp.bfloat16)
            dv_blk = dv_blk + lax.dot_general(
                prob_half, grad_blk, (((0,), (0,)), ((), ())), preferred_element_type=jnp.float32
            )
            dk_blk = dk_blk + score_scale * lax.dot_general(
                score_half, query_blk, (((0,), (0,)), ((), ())), preferred_element_type=jnp.float32
            )
            dq_blk = score_scale * jnp.dot(score_half, key_blk, preferred_element_type=jnp.float32)
            dq_all = lax.dynamic_update_slice(dq_all, dq_blk, (first_row, q_head * head_dim))
        old_key = lax.dynamic_slice(dk_ext, (0, key_start, 0), (1, key_span, head_dim))
        dk_ext = lax.dynamic_update_slice(dk_ext, old_key + dk_blk[None], (0, key_start, 0))
        old_value = lax.dynamic_slice(dv_ext, (0, key_start, 0), (1, key_span, head_dim))
        dv_ext = lax.dynamic_update_slice(dv_ext, old_value + dv_blk[None], (0, key_start, 0))
        return (dk_ext, dv_ext, dq_all)

    loop_carry = (
        jnp.zeros((kv_dev, ext_len, head_dim), jnp.float32),
        jnp.zeros((kv_dev, ext_len, head_dim), jnp.float32),
        jnp.zeros((seq_dev, heads_dev * head_dim), jnp.float32),
    )
    dk_ext, dv_ext, dq_all = lax.fori_loop(0, seq_dev // block_rows, block_step, loop_carry)
    grads_ext = jnp.stack([dk_ext, dv_ext], axis=0)
    total_kv = grads_ext[:, :, offset:, :]
    for distance in range(1, span_count + 1):
        far_part = grads_ext[
            :, :, offset - distance * seq_dev : offset - (distance - 1) * seq_dev, :
        ]
        total_kv = total_kv + shifted(far_part, "seq", -distance)
    kv_half = total_kv.astype(jnp.bfloat16)
    dk_cols = jnp.transpose(kv_half[0], (1, 0, 2)).reshape(seq_dev, kv_dev * head_dim)
    dv_cols = jnp.transpose(kv_half[1], (1, 0, 2)).reshape(seq_dev, kv_dev * head_dim)
    dq_cols = dq_all.astype(jnp.bfloat16)
    grad_query, key_gradient_rows, value_gradient_rows = (
        lax.all_to_all(dq_cols, "head", split_axis=0, concat_axis=1, tiled=True),
        lax.all_to_all(dk_cols, "head", split_axis=0, concat_axis=1, tiled=True),
        lax.all_to_all(dv_cols, "head", split_axis=0, concat_axis=1, tiled=True),
    )
    return (grad_query, key_gradient_rows, value_gradient_rows, grad_proj)


def solution(mesh):
    in_specs = (
        P(("seq", "head"), None),
        P("head", "seq", None),
        P(("seq", "head"), None),
        P(("seq", "head"), None),
        P("head", None),
        P("head", "seq", None),
        P("head", "seq", None),
        P("head", "seq", None),
        P("head", "seq", None),
        P("head", "seq"),
    )
    out_specs = (
        P(("seq", "head"), None),
        P(("seq", "head"), None),
        P(("seq", "head"), None),
        P("head", None),
    )
    return jax.shard_map(local, mesh=mesh, in_specs=in_specs, out_specs=out_specs, check_vma=False)
```

profile of v0, /device:TPU:6, one launch (start us, length us, event | category | flops | bytes accessed | tf_op | source)
XLA Modules:
  0.0 762.1 jit_solution(4666393536093147817)
XLA Ops:
  7.2 12.2 %copy.78 = bf16[1,512,6144]{2,0,1:T(2,128)(2,1)} copy(bf16[1,512,6144]{2,1,0:T(8,128)(2,1)} %param.13) | data formatting | bytes 12582912 | tf_op args[1]
  19.9 38.9 %reduce.2 = bf16[512,6144]{1,0:T(8,128)(2,1)} reduce(bf16[512,1,6144]{2,1,0:T(2,128)(2,1)} %bitcast.199, bf16[]{:T(256)} %broadcast.111), dimensions={1}, to_apply=%bitcast.134.reduce_sub_computation | reduce | bytes 12582914
  58.8 9.4 %reshape.158 = bf16[8,2,196608]{2,1,0:T(2,128)(2,1)} reshape(bf16[512,6144]{1,0:T(8,128)(2,1)} %reduce.2) | data formatting | bytes 12582912
  68.2 8.4 %all-to-all-start = ((bf16[8,2,196608]{2,1,0:T(2,128)(2,1)}), bf16[8,2,196608]{2,1,0:T(2,128)(2,1)}, u32[]{:S(2)}, u32[]{:S(2)}) async-start(bf16[8,2,196608]{2,1,0:T(2,128)(2,1)} %reshape.158), calls=%async_computation | async-start | bytes 12582912 | tf_op jit(solution)/shard_map/all_to_all | solution.py:46
  80.3 67.1 %all-to-all-done = bf16[8,2,196608]{2,1,0:T(2,128)(2,1)} async-done(((bf16[8,2,196608]{2,1,0:T(2,128)(2,1)}), bf16[8,2,196608]{2,1,0:T(2,128)(2,1)}, u32[]{:S(2)}, u32[]{:S(2)}) %all-to-all-start) | async-done | bytes 6291488 | tf_op jit(solution)/shard_map/all_to_all | solution.py:46
  147.4 11.0 %reshape.159 = bf16[512,1,6144]{2,1,0:T(2,128)(2,1)} reshape(bf16[8,2,196608]{2,1,0:T(2,128)(2,1)} %all-to-all-done) | data formatting | bytes 12582912
  158.4 11.0 %copy.77 = bf16[1,512,6144]{2,1,0:T(8,128)(2,1)} copy(bf16[1,512,6144]{2,0,1:T(2,128)(2,1)} %bitcast.198) | data formatting | bytes 12582912
  169.4 9.1 %gather_fusion = bf16[256,6144]{1,0:T(8,128)(2,1)S(1)} fusion(bf16[512,6144]{1,0:T(8,128)(2,1)} %bitcast.197, s32[1024]{0:T(1024)S(1)} %pad_clamp_fusion), kind=kCustom, calls=%fused_computation | custom fusion | bytes 6292480 | tf_op jit(solution)/shard_map/jit(_take)/gather | solution.py:26
  181.7 7.7 %copy.64 = bf16[128,2,6144]{0,2,1:T(8,128)(2,1)S(1)} copy(bf16[128,2,6144]{2,1,0:T(2,128)(2,1)} %gather.7) | data formatting | bytes 6291456 | tf_op jit(solution)/shard_map/jit(_take)/gather | solution.py:26
  205.2 13.0 %collective-permute-done = bf16[2,1,1024,128]{3,2,1,0:T(8,128)(2,1)} collective-permute-done((bf16[2,1,1024,128]{3,2,1,0:T(8,128)(2,1)}, bf16[2,1,1024,128]{3,2,1,0:T(8,128)(2,1)}, u32[]{:S(2)}, u32[]{:S(2)}) %collective-permute-start) | collective-permute-done | bytes 524320 | tf_op jit(solution)/shard_map/ppermute | solution.py:13
  219.3 8.6 %collective-permute-done.1 = bf16[2,1,1024,128]{3,2,1,0:T(8,128)(2,1)} collective-permute-done((bf16[2,1,1024,128]{3,2,1,0:T(8,128)(2,1)}, bf16[2,1,1024,128]{3,2,1,0:T(8,128)(2,1)}, u32[]{:S(2)}, u32[]{:S(2)}) %collective-permute-start.1) | collective-permute-done | bytes 524320 | tf_op jit(solution)/shard_map/ppermute | solution.py:13
  229.0 24.2 %collective-permute-done.2 = bf16[2,1,1024,128]{3,2,1,0:T(8,128)(2,1)} collective-permute-done((bf16[2,1,1024,128]{3,2,1,0:T(8,128)(2,1)}, bf16[2,1,1024,128]{3,2,1,0:T(8,128)(2,1)}, u32[]{:S(2)}, u32[]{:S(2)}) %collective-permute-start.2) | collective-permute-done | bytes 524320 | tf_op jit(solution)/shard_map/ppermute | solution.py:13
  257.6 103.3 %all-gather.2.cloned.1.call-done = bf16[1024,6144]{0,1:T(8,128)(2,1)} async-done(((bf16[128,6144]{0,1:T(8,128)(2,1)}), bf16[1024,6144]{0,1:T(8,128)(2,1)}) %all-gather.2.cloned.1.call-update) | async-done | bytes 12582928 | tf_op jit(solution)/shard_map/all_gather | solution.py:52
  360.9 10.1 %convolution_convert_fusion = bf16[1024,384]{0,1:T(8,128)(2,1)} fusion(bf16[384,6144]{1,0:T(8,128)(2,1)} %param.16, bf16[1024,6144]{0,1:T(8,128)(2,1)} %all-gather.2.cloned.1.call-done), kind=kOutput, calls=%fused_computation.121 | convolution fusion | flops 4832231424 | bytes 18087936 | tf_op jit(solution)/shard_map/dot_general | solution.py:53
  381.5 99.3 %while.20 = (s32[]{:T(128)}, f32[1,5120,128]{2,1,0:T(8,128)}, f32[1,5120,128]{2,1,0:T(8,128)}, bf16[1024,384]{1,0:T(8,128)(2,1)}, s32[]{:T(128)}, /*index=5*/bf1...) while((s32[]{:T(128)}, f32[1,5120,128]{2,1,0:T(8,128)}, ...), condition=%wide.region_5.6_spmd.clone, body=%wide.region_4.5_spmd.clone.sunk | while | flops 9156034560 | bytes 252151056 | solution.py:131
  495.3 7.1 all-to-all-start.1
  502.4 23.6 %collective-permute-done.4 = f32[2,1,1024,128]{3,2,1,0:T(8,128)S(1)} collective-permute-done((f32[2,1,1024,128]{3,2,1,0:T(8,128)}, f32[2,1,1024,128]{3,2,1,0:T(8,128)S(1)}, u32[]{:S(2)}, u32[]{:S(2)}) %collective-permute-start.4) | collective-permute-done | bytes 1048608 | tf_op jit(solution)/shard_map/ppermute | solution.py:13
  525.9 30.3 %collective-permute-done.5 = f32[2,1,1024,128]{3,2,1,0:T(8,128)} collective-permute-done((f32[2,1,1024,128]{3,2,1,0:T(8,128)}, f32[2,1,1024,128]{3,2,1,0:T(8,128)}, u32[]{:S(2)}, u32[]{:S(2)}) %collective-permute-start.5) | collective-permute-done | bytes 1048608 | tf_op jit(solution)/shard_map/ppermute | solution.py:13
  556.2 22.5 %collective-permute-done.7 = f32[2,1,1024,128]{3,2,1,0:T(8,128)} collective-permute-done((f32[2,1,1024,128]{3,2,1,0:T(8,128)}, f32[2,1,1024,128]{3,2,1,0:T(8,128)}, u32[]{:S(2)}, u32[]{:S(2)}) %collective-permute-start.7) | collective-permute-done | bytes 1048608 | tf_op jit(solution)/shard_map/ppermute | solution.py:13
  578.7 17.8 %collective-permute-done.6 = f32[2,1,1024,128]{3,2,1,0:T(8,128)} collective-permute-done((f32[2,1,1024,128]{3,2,1,0:T(8,128)S(1)}, f32[2,1,1024,128]{3,2,1,0:T(8,128)}, u32[]{:S(2)}, u32[]{:S(2)}) %collective-permute-start.6) | collective-permute-done | bytes 1048608 | tf_op jit(solution)/shard_map/ppermute | solution.py:13
  612.2 11.8 %fusion.95 = f32[3,128,6144]{1,2,0:T(8,128)} fusion(bf16[3,1024,128]{2,1,0:T(8,128)(2,1)S(1)} %copy-done.16, bf16[1024,6144]{0,1:T(8,128)(2,1)} %all-gather.2.cloned.1.call-done), kind=kOutput, calls=%fused_computation.101 | convolution fusion | flops 4831838208 | bytes 22806528 | tf_op jit(solution)/shard_map/dot_general | solution.py:56
  624.0 7.2 all-to-all-start.3
  631.2 113.4 %all-reduce.1 = bf16[3,128,6144]{1,2,0:T(8,128)(2,1)} all-reduce(f32[3,128,6144]{1,2,0:T(8,128)} %fusion.95), channel_id=1, replica_groups=mesh['seq'=16,'head'=8] {'seq'}, use_global_device_ids=true, to_apply=%region_6.7 | all-reduce | flops 2359296 | bytes 14155776 | tf_op jit(solution)/shard_map/psum | solution.py:60
  744.6 6.6 copy.70
  (192 shorter events, 172.4 us)
Async XLA Ops:
  68.2 8.4 %copy-start.18 = (s32[128,2]{0,1:T(2,128)S(1)}, s32[128,2]{0,1:T(2,128)}, u32[]{:S(2)}) copy-start(s32[128,2]{0,1:T(2,128)} %param.14) | copy-start | bytes 3076
  68.2 10.5 %copy-start.13 = (bf16[128,6144]{1,0:T(8,128)(2,1)S(1)}, bf16[128,6144]{1,0:T(8,128)(2,1)}, u32[]{:S(2)}) copy-start(bf16[128,6144]{1,0:T(8,128)(2,1)} %param.12) | copy-start | bytes 4718596
  68.2 79.2 %all-to-all-start = ((bf16[8,2,196608]{2,1,0:T(2,128)(2,1)}), bf16[8,2,196608]{2,1,0:T(2,128)(2,1)}, u32[]{:S(2)}, u32[]{:S(2)}) async-start(bf16[8,2,196608]{2,1,0:T(2,128)(2,1)} %reshape.158), calls=%async_computation | async-start | bytes 12582912 | tf_op jit(solution)/shard_map/all_to_all | solution.py:46
  76.6 284.3 %all-gather.2.cloned.1.call-start = ((), (), s32[]{:S(2)}) async-start(), calls=%async_computation.4 | async-start | bytes 14155776 | tf_op jit(solution)/shard_map/all_gather | solution.py:52
  193.7 24.5 %collective-permute-start = (bf16[2,1,1024,128]{3,2,1,0:T(8,128)(2,1)}, bf16[2,1,1024,128]{3,2,1,0:T(8,128)(2,1)}, u32[]{:S(2)}, u32[]{:S(2)}) collective-permute-start(bf16[2,1,1024,128]{3,2,1,0:T(8,128)(2,1)} %pad_maximum_fusion.1), channel_id=1, source_target_pairs={{0,32},{8,40},{16,48},{24,56},{32,64},{40,72},{48,80},{56,88},{64,... | collective-permute-start | bytes 1572872 | tf_op jit(solution)/shard_map/ppermute | solution.py:13
  198.8 29.1 %collective-permute-start.1 = (bf16[2,1,1024,128]{3,2,1,0:T(8,128)(2,1)}, bf16[2,1,1024,128]{3,2,1,0:T(8,128)(2,1)}, u32[]{:S(2)}, u32[]{:S(2)}) collective-permute-start(bf16[2,1,1024,128]{3,2,1,0:T(8,128)(2,1)} %pad_maximum_fusion.1), channel_id=1, source_target_pairs={{0,24},{8,32},{16,40},{24,48},{32,56},{40,64},{48,72},{56,80},{64,... | collective-permute-start | bytes 1572872 | tf_op jit(solution)/shard_map/ppermute | solution.py:13
  200.7 52.5 %collective-permute-start.2 = (bf16[2,1,1024,128]{3,2,1,0:T(8,128)(2,1)}, bf16[2,1,1024,128]{3,2,1,0:T(8,128)(2,1)}, u32[]{:S(2)}, u32[]{:S(2)}) collective-permute-start(bf16[2,1,1024,128]{3,2,1,0:T(8,128)(2,1)} %pad_maximum_fusion.1), channel_id=1, source_target_pairs={{0,16},{8,24},{16,32},{24,40},{32,48},{40,56},{48,64},{56,72},{64,... | collective-permute-start | bytes 1572872 | tf_op jit(solution)/shard_map/ppermute | solution.py:13
  203.3 53.1 %collective-permute-start.3 = (bf16[2,1,1024,128]{3,2,1,0:T(8,128)(2,1)}, bf16[2,1,1024,128]{3,2,1,0:T(8,128)(2,1)}, u32[]{:S(2)}, u32[]{:S(2)}) collective-permute-start(bf16[2,1,1024,128]{3,2,1,0:T(8,128)(2,1)} %pad_maximum_fusion.1), channel_id=1, source_target_pairs={{0,8},{8,16},{16,24},{24,32},{32,40},{40,48},{48,56},{56,64},{64,7... | collective-permute-start | bytes 1572872 | tf_op jit(solution)/shard_map/ppermute | solution.py:13
  381.7 14.1 %copy-start.5 = (bf16[1024,384]{1,0:T(8,128)(2,1)}, bf16[1024,384]{1,0:T(8,128)(2,1)S(1)}, u32[]{:S(2)}) copy-start(bf16[1024,384]{1,0:T(8,128)(2,1)S(1)} %get-tuple-element.567) | copy-start | bytes 2359300 | tf_op jit(solution)/shard_map/while
  384.3 7.6 %copy-start.9 = (bf16[1,1024,128]{2,1,0:T(8,128)(2,1)}, bf16[1,1024,128]{2,1,0:T(8,128)(2,1)S(1)}, u32[]{:S(2)}) copy-start(bf16[1,1024,128]{2,1,0:T(8,128)(2,1)S(1)} %get-tuple-element.520) | copy-start | bytes 786436 | tf_op jit(solution)/shard_map/while
  384.5 11.3 %copy-start = (bf16[1,1,5120,128]{3,2,1,0:T(8,128)(2,1)}, bf16[1,1,5120,128]{3,2,1,0:T(8,128)(2,1)S(1)}, u32[]{:S(2)}) copy-start(bf16[1,1,5120,128]{3,2,1,0:T(8,128)(2,1)S(1)} %get-tuple-element.518) | copy-start | bytes 3932164 | tf_op jit(solution)/shard_map/while
  409.4 11.4 %slice-start.2 = ((s8[4718592]{0:T(1024)(128)(4,1)}), s8[4194304]{0:T(1024)(128)(4,1)S(1)}, s32[]{:S(2)}) async-start(s8[4718592]{0:T(1024)(128)(4,1)} %bitcast.195), calls=%async_computation.7 | async-start | bytes 8388608 | tf_op jit(solution)/shard_map/while
  431.1 14.1 %copy-start.5 = (bf16[1024,384]{1,0:T(8,128)(2,1)}, bf16[1024,384]{1,0:T(8,128)(2,1)S(1)}, u32[]{:S(2)}) copy-start(bf16[1024,384]{1,0:T(8,128)(2,1)S(1)} %get-tuple-element.567) | copy-start | bytes 2359300 | tf_op jit(solution)/shard_map/while
  433.7 7.6 %copy-start.9 = (bf16[1,1024,128]{2,1,0:T(8,128)(2,1)}, bf16[1,1024,128]{2,1,0:T(8,128)(2,1)S(1)}, u32[]{:S(2)}) copy-start(bf16[1,1024,128]{2,1,0:T(8,128)(2,1)S(1)} %get-tuple-element.520) | copy-start | bytes 786436 | tf_op jit(solution)/shard_map/while
  433.9 11.3 %copy-start = (bf16[1,1,5120,128]{3,2,1,0:T(8,128)(2,1)}, bf16[1,1,5120,128]{3,2,1,0:T(8,128)(2,1)S(1)}, u32[]{:S(2)}) copy-start(bf16[1,1,5120,128]{3,2,1,0:T(8,128)(2,1)S(1)} %get-tuple-element.518) | copy-start | bytes 3932164 | tf_op jit(solution)/shard_map/while
  458.8 11.4 %slice-start.2 = ((s8[4718592]{0:T(1024)(128)(4,1)}), s8[4194304]{0:T(1024)(128)(4,1)S(1)}, s32[]{:S(2)}) async-start(s8[4718592]{0:T(1024)(128)(4,1)} %bitcast.195), calls=%async_computation.7 | async-start | bytes 8388608 | tf_op jit(solution)/shard_map/while
  484.7 41.3 %collective-permute-start.4 = (f32[2,1,1024,128]{3,2,1,0:T(8,128)}, f32[2,1,1024,128]{3,2,1,0:T(8,128)S(1)}, u32[]{:S(2)}, u32[]{:S(2)}) collective-permute-start(f32[2,1,1024,128]{3,2,1,0:T(8,128)} %get-tuple-element.420), channel_id=1, source_target_pairs={{8,0},{16,8},{24,16},{32,24},{40,32},{48,40},{56,48},{64,56},{72,6... | collective-permute-start | bytes 3145736 | tf_op jit(solution)/shard_map/ppermute | solution.py:13
  487.8 68.4 %collective-permute-start.5 = (f32[2,1,1024,128]{3,2,1,0:T(8,128)}, f32[2,1,1024,128]{3,2,1,0:T(8,128)}, u32[]{:S(2)}, u32[]{:S(2)}) collective-permute-start(f32[2,1,1024,128]{3,2,1,0:T(8,128)} %get-tuple-element.421), channel_id=1, source_target_pairs={{16,0},{24,8},{32,16},{40,24},{48,32},{56,40},{64,48},{72,56},{80,... | collective-permute-start | bytes 3145736 | tf_op jit(solution)/shard_map/ppermute | solution.py:13
  490.6 88.0 %collective-permute-start.7 = (f32[2,1,1024,128]{3,2,1,0:T(8,128)}, f32[2,1,1024,128]{3,2,1,0:T(8,128)}, u32[]{:S(2)}, u32[]{:S(2)}) collective-permute-start(f32[2,1,1024,128]{3,2,1,0:T(8,128)} %get-tuple-element.422), channel_id=1, source_target_pairs={{32,0},{40,8},{48,16},{56,24},{64,32},{72,40},{80,48},{88,56},{96,... | collective-permute-start | bytes 3145736 | tf_op jit(solution)/shard_map/ppermute | solution.py:13
  493.4 103.1 %collective-permute-start.6 = (f32[2,1,1024,128]{3,2,1,0:T(8,128)S(1)}, f32[2,1,1024,128]{3,2,1,0:T(8,128)}, u32[]{:S(2)}, u32[]{:S(2)}) collective-permute-start(f32[2,1,1024,128]{3,2,1,0:T(8,128)S(1)} %get-tuple-element.423), channel_id=1, source_target_pairs={{24,0},{32,8},{40,16},{48,24},{56,32},{64,40},{72,48},{80,56},{88,... | collective-permute-start | bytes 3145736 | tf_op jit(solution)/shard_map/ppermute | solution.py:13
  495.3 110.8 %all-to-all-start.1 = ((bf16[8,128,384]{2,1,0:T(8,128)(2,1)}), bf16[8,128,384]{2,1,0:T(8,128)(2,1)S(1)}, u32[]{:S(2)}, u32[]{:S(2)}) async-start(bf16[8,128,384]{2,1,0:T(8,128)(2,1)} %bitcast.12), calls=%async_computation.1 | async-start | bytes 1572864 | tf_op jit(solution)/shard_map/all_to_all | solution.py:144
  596.5 15.7 %copy-start.16 = (bf16[3,1024,128]{2,1,0:T(8,128)(2,1)S(1)}, bf16[3,1024,128]{2,1,0:T(8,128)(2,1)}, u32[]{:S(2)}) copy-start(bf16[3,1024,128]{2,1,0:T(8,128)(2,1)} %param.17) | copy-start | bytes 2359300
  606.1 17.9 %all-to-all-start.2 = ((bf16[8,128,128]{2,1,0:T(8,128)(2,1)}), bf16[8,128,128]{2,1,0:T(8,128)(2,1)S(1)}, u32[]{:S(2)}, u32[]{:S(2)}) async-start(bf16[8,128,128]{2,1,0:T(8,128)(2,1)} %bitcast.17), calls=%async_computation.2 | async-start | bytes 524288 | tf_op jit(solution)/shard_map/all_to_all | solution.py:145
  624.0 129.8 %all-to-all-start.3 = ((bf16[8,128,128]{2,1,0:T(8,128)(2,1)}), bf16[8,128,128]{2,1,0:T(8,128)(2,1)S(1)}, u32[]{:S(2)}, u32[]{:S(2)}) async-start(bf16[8,128,128]{2,1,0:T(8,128)(2,1)} %bitcast.20), calls=%async_computation.3 | async-start | bytes 524288 | tf_op jit(solution)/shard_map/all_to_all | solution.py:146
  (29 other events, 107.9 us)
Sparse Core Ops, SparseCore 0:
  192.9 167.9 all-gather.1
where the time goes:
time: 768 us; the launch traced here: 762 us
  waiting for transfers between devices  319 us (42%)
  matrix products  115 us (15%)
  blocking collectives  113 us (15%)
  local copies, waits for them, and re-layouts  97.2 us (13%)
  other arithmetic  51.5 us (7%)
  starting transfers between devices  50.8 us (7%)
  between operations  14.7 us (2%)
    ppermute x8, waiting for transfers between devices, shifted(): return lax.ppermute(block, axis, route)  142 us
    psum x1, blocking collectives, local(): summed_proj = lax.psum(partial_value, 'seq')  113 us
    all_gather x1, waiting for transfers between devices, local(): piece = lax.all_gather(hidden, 'head', axis=0, tiled=True)  103 us
    all_to_all x1, waiting for transfers between devices, local(): lax.all_to_all(expert_rows, 'head', split_axis=1, concat_axis=0, tiled=True)  67.1 us
    unnamed x31, local copies, waits for them, and re-layouts  55.6 us
    unnamed x1, other arithmetic  38.9 us
    dot_general x6, matrix products, block_step(): lax.dot_general(query_blk, key_blk, (((1,), (1,)), ((), ())), preferred_e...  25.6 us
    ppermute x8, starting transfers between devices, shifted(): return lax.ppermute(block, axis, route)  22.1 us
  transfers between devices with their start and end apart: 13, of which 11 were waited for; matrix products, arithmetic and copies ran while one was open for 4% of the time, Pallas kernels for 0%

commit v1 on v0

--- a/solution.py
+++ b/solution.py
@@ -1,3 +1,4 @@
+import functools
 import math
 import jax
 import jax.numpy as jnp
@@ -5,6 +6,14 @@
 from jax.sharding import PartitionSpec as P
 
 WIN = 4096
+
+
+def build_roots_by_axis(state, net_axis):
+    x_new = jnp.stack(jnp.split(state, lax.axis_size(net_axis), axis=1), axis=0)
+    return jnp.concatenate(lax.all_to_all(x_new, net_axis, 0, 0), axis=0)
+
+
+find_field_in = functools.partial(build_roots_by_axis, net_axis="head")
 
 
 def shifted(block, axis, distance):
@@ -43,7 +52,7 @@
     kv_dev = saved_keys.shape[0]
     group_size = heads_dev // kv_dev
     model_width = out_grad.shape[1]
-    returned = lax.all_to_all(expert_rows, "head", split_axis=1, concat_axis=0, tiled=True)
+    returned = find_field_in(expert_rows)
     picked = routed_rows(returned, expert_ids)
     summed = out_grad.astype(jnp.float32)
     summed = summed + gates[:, 0:1] * picked[:, 0].astype(jnp.float32)

time: 768 us -> 722 us (0.940)
  other arithmetic: 51.5 us -> 12.4 us
  local copies, waits for them, and re-layouts: 97.2 us -> 69.3 us
  loops' own time: 0.85 us -> 18.6 us
    unnamed x1 -> x0, other arithmetic: 38.9 us -> none
    unnamed x31 -> x33, local copies, waits for them, and re-layouts: 55.6 us -> 26.1 us
    another operation x1, loops' own time: 0.85 us -> 18.6 us  [local(): lax.fori_loop(0, seq_dev // block_rows, block_step, loop_carry)]
  transfers between devices with their start and end apart: 13 -> 13, of which waited for: 11 -> 11; matrix products, arithmetic and copies ran while one was open for 4% -> 5% of each run, Pallas kernels for 0% -> 0%
where the time goes in v1:
time: 722 us; the launch traced here: 713 us
  waiting for transfers between devices  319 us (44%)
  matrix products  115 us (16%)
  blocking collectives  113 us (16%)
  local copies, waits for them, and re-layouts  69.3 us (10%)
  starting transfers between devices  51.2 us (7%)
  loops' own time  18.6 us (3%)
  between operations  14.7 us (2%)
  other arithmetic  12.4 us (2%)
    ppermute x8, waiting for transfers between devices, shifted(): return lax.ppermute(block, axis, route)  142 us
    psum x1, blocking collectives, local(): summed_proj = lax.psum(partial_value, 'seq')  113 us
    all_gather x1, waiting for transfers between devices, local(): piece = lax.all_gather(hidden, 'head', axis=0, tiled=True)  103 us
    all_to_all x1, waiting for transfers between devices, build_roots_by_axis(): return jnp.concatenate(lax.all_to_all(x_new, net_axis, 0, 0), axis=0)  67.3 us
    unnamed x33, local copies, waits for them, and re-layouts  26.1 us
    dot_general x6, matrix products, block_step(): lax.dot_general(query_blk, key_blk, (((1,), (1,)), ((), ())), preferred_e...  25.6 us
    ppermute x8, starting transfers between devices, shifted(): return lax.ppermute(block, axis, route)  22.4 us
    dot_general x6, matrix products, block_step(): lax.dot_general(grad_blk, value_blk, (((1,), (1,)), ((), ())), preferred_...  20.5 us
  transfers between devices with their start and end apart: 13, of which 11 were waited for; matrix products, arithmetic and copies ran while one was open for 5% of the time, Pallas kernels for 0%

profile of v1, /device:TPU:6, one launch (start us, length us, event | category | flops | bytes accessed | tf_op | source)
XLA Modules:
  0.0 713.1 jit_solution(18419546368677947312)
XLA Ops:
  23.8 8.4 %all-to-all-start = ((bf16[8,1,64,6144]{3,2,1,0:T(8,128)(2,1)}), bf16[8,1,64,6144]{3,2,1,0:T(8,128)(2,1)}, u32[]{:S(2)}, u32[]{:S(2)}) async-start(bf16[8,1,64,6144]{3,2,1,0:T(8,128)(2,1)} %bitcast_dynamic-update-slice_fusion), calls=%async_computation | async-start | bytes 12582912 | tf_op jit(solution)/shard_map/all_to_all | solution.py:13
  35.7 67.3 %all-to-all-done = bf16[8,1,64,6144]{3,2,1,0:T(8,128)(2,1)} async-done(((bf16[8,1,64,6144]{3,2,1,0:T(8,128)(2,1)}), bf16[8,1,64,6144]{3,2,1,0:T(8,128)(2,1)}, u32[]{:S(2)}, u32[]{:S(2)}) %all-to-all-start) | async-done | bytes 6291488 | tf_op jit(solution)/shard_map/all_to_all | solution.py:13
  103.0 9.1 %gather_fusion = bf16[256,6144]{1,0:T(8,128)(2,1)S(1)} fusion(bf16[512,6144]{1,0:T(8,128)(2,1)} %bitcast.13, s32[1024]{0:T(1024)S(1)} %pad_clamp_fusion), kind=kCustom, calls=%fused_computation | custom fusion | bytes 6292480 | tf_op jit(solution)/shard_map/jit(_take)/gather | solution.py:35
  115.4 7.2 %copy.61 = bf16[128,2,6144]{0,2,1:T(8,128)(2,1)S(1)} copy(bf16[128,2,6144]{2,1,0:T(2,128)(2,1)} %gather.7) | data formatting | bytes 6291456 | tf_op jit(solution)/shard_map/jit(_take)/gather | solution.py:35
  126.9 5.1 collective-permute-start
  138.7 12.7 %collective-permute-done = bf16[2,1,1024,128]{3,2,1,0:T(8,128)(2,1)} collective-permute-done((bf16[2,1,1024,128]{3,2,1,0:T(8,128)(2,1)}, bf16[2,1,1024,128]{3,2,1,0:T(8,128)(2,1)}, u32[]{:S(2)}, u32[]{:S(2)}) %collective-permute-start) | collective-permute-done | bytes 524320 | tf_op jit(solution)/shard_map/ppermute | solution.py:22
  152.5 8.6 %collective-permute-done.1 = bf16[2,1,1024,128]{3,2,1,0:T(8,128)(2,1)} collective-permute-done((bf16[2,1,1024,128]{3,2,1,0:T(8,128)(2,1)}, bf16[2,1,1024,128]{3,2,1,0:T(8,128)(2,1)}, u32[]{:S(2)}, u32[]{:S(2)}) %collective-permute-start.1) | collective-permute-done | bytes 524320 | tf_op jit(solution)/shard_map/ppermute | solution.py:22
  162.2 24.2 %collective-permute-done.2 = bf16[2,1,1024,128]{3,2,1,0:T(8,128)(2,1)} collective-permute-done((bf16[2,1,1024,128]{3,2,1,0:T(8,128)(2,1)}, bf16[2,1,1024,128]{3,2,1,0:T(8,128)(2,1)}, u32[]{:S(2)}, u32[]{:S(2)}) %collective-permute-start.2) | collective-permute-done | bytes 524320 | tf_op jit(solution)/shard_map/ppermute | solution.py:22
  190.8 103.3 %all-gather.2.cloned.1.call-done = bf16[1024,6144]{0,1:T(8,128)(2,1)} async-done(((bf16[128,6144]{0,1:T(8,128)(2,1)}), bf16[1024,6144]{0,1:T(8,128)(2,1)}) %all-gather.2.cloned.1.call-update) | async-done | bytes 12582928 | tf_op jit(solution)/shard_map/all_gather | solution.py:61
  294.1 10.1 %convolution_convert_fusion = bf16[1024,384]{0,1:T(8,128)(2,1)} fusion(bf16[384,6144]{1,0:T(8,128)(2,1)} %param.16, bf16[1024,6144]{0,1:T(8,128)(2,1)} %all-gather.2.cloned.1.call-done), kind=kOutput, calls=%fused_computation.120 | convolution fusion | flops 4832231424 | bytes 18087936 | tf_op jit(solution)/shard_map/dot_general | solution.py:62
  314.7 116.9 %while.20 = (s32[]{:T(128)}, f32[1,5120,128]{2,1,0:T(8,128)}, f32[1,5120,128]{2,1,0:T(8,128)}, bf16[1024,384]{1,0:T(8,128)(2,1)}, s32[]{:T(128)}, /*index=5*/bf1...) while((s32[]{:T(128)}, f32[1,5120,128]{2,1,0:T(8,128)}, ...), condition=%wide.region_5.6_spmd.clone, body=%wide.region_4.5_spmd.clone.sunk | while | flops 9156034560 | bytes 252151056 | solution.py:140
  350.4 5.2 exponential_select_fusion.6
  399.8 5.2 exponential_select_fusion.6
  446.2 7.0 all-to-all-start.1
  453.2 23.5 %collective-permute-done.4 = f32[2,1,1024,128]{3,2,1,0:T(8,128)S(1)} collective-permute-done((f32[2,1,1024,128]{3,2,1,0:T(8,128)}, f32[2,1,1024,128]{3,2,1,0:T(8,128)S(1)}, u32[]{:S(2)}, u32[]{:S(2)}) %collective-permute-start.4) | collective-permute-done | bytes 1048608 | tf_op jit(solution)/shard_map/ppermute | solution.py:22
  476.7 30.3 %collective-permute-done.5 = f32[2,1,1024,128]{3,2,1,0:T(8,128)} collective-permute-done((f32[2,1,1024,128]{3,2,1,0:T(8,128)}, f32[2,1,1024,128]{3,2,1,0:T(8,128)}, u32[]{:S(2)}, u32[]{:S(2)}) %collective-permute-start.5) | collective-permute-done | bytes 1048608 | tf_op jit(solution)/shard_map/ppermute | solution.py:22
  507.1 22.5 %collective-permute-done.7 = f32[2,1,1024,128]{3,2,1,0:T(8,128)} collective-permute-done((f32[2,1,1024,128]{3,2,1,0:T(8,128)}, f32[2,1,1024,128]{3,2,1,0:T(8,128)}, u32[]{:S(2)}, u32[]{:S(2)}) %collective-permute-start.7) | collective-permute-done | bytes 1048608 | tf_op jit(solution)/shard_map/ppermute | solution.py:22
  529.5 17.9 %collective-permute-done.6 = f32[2,1,1024,128]{3,2,1,0:T(8,128)} collective-permute-done((f32[2,1,1024,128]{3,2,1,0:T(8,128)S(1)}, f32[2,1,1024,128]{3,2,1,0:T(8,128)}, u32[]{:S(2)}, u32[]{:S(2)}) %collective-permute-start.6) | collective-permute-done | bytes 1048608 | tf_op jit(solution)/shard_map/ppermute | solution.py:22
  550.7 6.4 all-to-all-done.1
  557.0 6.2 all-to-all-start.2
  563.2 11.8 %fusion.95 = f32[3,128,6144]{1,2,0:T(8,128)} fusion(bf16[3,1024,128]{2,1,0:T(8,128)(2,1)S(1)} %copy-done.16, bf16[1024,6144]{0,1:T(8,128)(2,1)} %all-gather.2.cloned.1.call-done), kind=kOutput, calls=%fused_computation.101 | convolution fusion | flops 4831838208 | bytes 22806528 | tf_op jit(solution)/shard_map/dot_general | solution.py:65
  575.0 7.2 %all-to-all-start.3 = ((bf16[8,128,128]{2,1,0:T(8,128)(2,1)}), bf16[8,128,128]{2,1,0:T(8,128)(2,1)S(1)}, u32[]{:S(2)}, u32[]{:S(2)}) async-start(bf16[8,128,128]{2,1,0:T(8,128)(2,1)} %bitcast.29), calls=%async_computation.3 | async-start | bytes 524288 | tf_op jit(solution)/shard_map/all_to_all | solution.py:155
  582.2 113.4 %all-reduce.1 = bf16[3,128,6144]{1,2,0:T(8,128)(2,1)} all-reduce(f32[3,128,6144]{1,2,0:T(8,128)} %fusion.95), channel_id=1, replica_groups=mesh['seq'=16,'head'=8] {'seq'}, use_global_device_ids=true, to_apply=%region_6.7 | all-reduce | flops 2359296 | bytes 14155776 | tf_op jit(solution)/shard_map/psum | solution.py:69
  695.6 6.6 copy.67
  (194 shorter events, 160.7 us)
Async XLA Ops:
  23.8 8.4 %copy-start.18 = (s32[128,2]{0,1:T(2,128)S(1)}, s32[128,2]{0,1:T(2,128)}, u32[]{:S(2)}) copy-start(s32[128,2]{0,1:T(2,128)} %param.14) | copy-start | bytes 3076
  23.8 10.2 %copy-start.13 = (bf16[128,6144]{1,0:T(8,128)(2,1)S(1)}, bf16[128,6144]{1,0:T(8,128)(2,1)}, u32[]{:S(2)}) copy-start(bf16[128,6144]{1,0:T(8,128)(2,1)} %param.12) | copy-start | bytes 4718596
  23.8 11.9 %copy-start.19 = (f32[128,2]{0,1:T(2,128)S(1)}, f32[128,2]{0,1:T(2,128)}, u32[]{:S(2)}) copy-start(f32[128,2]{0,1:T(2,128)} %param.15) | copy-start | bytes 3076
  23.8 79.2 %all-to-all-start = ((bf16[8,1,64,6144]{3,2,1,0:T(8,128)(2,1)}), bf16[8,1,64,6144]{3,2,1,0:T(8,128)(2,1)}, u32[]{:S(2)}, u32[]{:S(2)}) async-start(bf16[8,1,64,6144]{3,2,1,0:T(8,128)(2,1)} %bitcast_dynamic-update-slice_fusion), calls=%async_computation | async-start | bytes 12582912 | tf_op jit(solution)/shard_map/all_to_all | solution.py:13
  32.2 261.9 %all-gather.2.cloned.1.call-start = ((), (), s32[]{:S(2)}) async-start(), calls=%async_computation.4 | async-start | bytes 14155776 | tf_op jit(solution)/shard_map/all_gather | solution.py:61
  126.9 24.5 %collective-permute-start = (bf16[2,1,1024,128]{3,2,1,0:T(8,128)(2,1)}, bf16[2,1,1024,128]{3,2,1,0:T(8,128)(2,1)}, u32[]{:S(2)}, u32[]{:S(2)}) collective-permute-start(bf16[2,1,1024,128]{3,2,1,0:T(8,128)(2,1)} %pad_maximum_fusion.1), channel_id=1, source_target_pairs={{0,32},{8,40},{16,48},{24,56},{32,64},{40,72},{48,80},{56,88},{64,... | collective-permute-start | bytes 1572872 | tf_op jit(solution)/shard_map/ppermute | solution.py:22
  132.0 29.1 %collective-permute-start.1 = (bf16[2,1,1024,128]{3,2,1,0:T(8,128)(2,1)}, bf16[2,1,1024,128]{3,2,1,0:T(8,128)(2,1)}, u32[]{:S(2)}, u32[]{:S(2)}) collective-permute-start(bf16[2,1,1024,128]{3,2,1,0:T(8,128)(2,1)} %pad_maximum_fusion.1), channel_id=1, source_target_pairs={{0,24},{8,32},{16,40},{24,48},{32,56},{40,64},{48,72},{56,80},{64,... | collective-permute-start | bytes 1572872 | tf_op jit(solution)/shard_map/ppermute | solution.py:22
  133.9 52.5 %collective-permute-start.2 = (bf16[2,1,1024,128]{3,2,1,0:T(8,128)(2,1)}, bf16[2,1,1024,128]{3,2,1,0:T(8,128)(2,1)}, u32[]{:S(2)}, u32[]{:S(2)}) collective-permute-start(bf16[2,1,1024,128]{3,2,1,0:T(8,128)(2,1)} %pad_maximum_fusion.1), channel_id=1, source_target_pairs={{0,16},{8,24},{16,32},{24,40},{32,48},{40,56},{48,64},{56,72},{64,... | collective-permute-start | bytes 1572872 | tf_op jit(solution)/shard_map/ppermute | solution.py:22
  136.5 53.1 %collective-permute-start.3 = (bf16[2,1,1024,128]{3,2,1,0:T(8,128)(2,1)}, bf16[2,1,1024,128]{3,2,1,0:T(8,128)(2,1)}, u32[]{:S(2)}, u32[]{:S(2)}) collective-permute-start(bf16[2,1,1024,128]{3,2,1,0:T(8,128)(2,1)} %pad_maximum_fusion.1), channel_id=1, source_target_pairs={{0,8},{8,16},{16,24},{24,32},{32,40},{40,48},{48,56},{56,64},{64,7... | collective-permute-start | bytes 1572872 | tf_op jit(solution)/shard_map/ppermute | solution.py:22
  332.6 14.1 %copy-start.5 = (bf16[1024,384]{1,0:T(8,128)(2,1)}, bf16[1024,384]{1,0:T(8,128)(2,1)S(1)}, u32[]{:S(2)}) copy-start(bf16[1024,384]{1,0:T(8,128)(2,1)S(1)} %get-tuple-element.567) | copy-start | bytes 2359300 | tf_op jit(solution)/shard_map/while
  335.2 7.7 %copy-start.9 = (bf16[1,1024,128]{2,1,0:T(8,128)(2,1)}, bf16[1,1024,128]{2,1,0:T(8,128)(2,1)S(1)}, u32[]{:S(2)}) copy-start(bf16[1,1024,128]{2,1,0:T(8,128)(2,1)S(1)} %get-tuple-element.520) | copy-start | bytes 786436 | tf_op jit(solution)/shard_map/while
  335.4 11.3 %copy-start = (bf16[1,1,5120,128]{3,2,1,0:T(8,128)(2,1)}, bf16[1,1,5120,128]{3,2,1,0:T(8,128)(2,1)S(1)}, u32[]{:S(2)}) copy-start(bf16[1,1,5120,128]{3,2,1,0:T(8,128)(2,1)S(1)} %get-tuple-element.518) | copy-start | bytes 3932164 | tf_op jit(solution)/shard_map/while
  360.3 11.4 %slice-start.2 = ((s8[4718592]{0:T(1024)(128)(4,1)}), s8[4194304]{0:T(1024)(128)(4,1)S(1)}, s32[]{:S(2)}) async-start(s8[4718592]{0:T(1024)(128)(4,1)} %bitcast.205), calls=%async_computation.7 | async-start | bytes 8388608 | tf_op jit(solution)/shard_map/while
  382.1 14.1 %copy-start.5 = (bf16[1024,384]{1,0:T(8,128)(2,1)}, bf16[1024,384]{1,0:T(8,128)(2,1)S(1)}, u32[]{:S(2)}) copy-start(bf16[1024,384]{1,0:T(8,128)(2,1)S(1)} %get-tuple-element.567) | copy-start | bytes 2359300 | tf_op jit(solution)/shard_map/while
  384.8 11.3 %copy-start = (bf16[1,1,5120,128]{3,2,1,0:T(8,128)(2,1)}, bf16[1,1,5120,128]{3,2,1,0:T(8,128)(2,1)S(1)}, u32[]{:S(2)}) copy-start(bf16[1,1,5120,128]{3,2,1,0:T(8,128)(2,1)S(1)} %get-tuple-element.518) | copy-start | bytes 3932164 | tf_op jit(solution)/shard_map/while
  409.7 11.4 %slice-start.2 = ((s8[4718592]{0:T(1024)(128)(4,1)}), s8[4194304]{0:T(1024)(128)(4,1)S(1)}, s32[]{:S(2)}) async-start(s8[4718592]{0:T(1024)(128)(4,1)} %bitcast.205), calls=%async_computation.7 | async-start | bytes 8388608 | tf_op jit(solution)/shard_map/while
  435.6 41.2 %collective-permute-start.4 = (f32[2,1,1024,128]{3,2,1,0:T(8,128)}, f32[2,1,1024,128]{3,2,1,0:T(8,128)S(1)}, u32[]{:S(2)}, u32[]{:S(2)}) collective-permute-start(f32[2,1,1024,128]{3,2,1,0:T(8,128)} %get-tuple-element.420), channel_id=1, source_target_pairs={{8,0},{16,8},{24,16},{32,24},{40,32},{48,40},{56,48},{64,56},{72,6... | collective-permute-start | bytes 3145736 | tf_op jit(solution)/shard_map/ppermute | solution.py:22
  438.6 68.4 %collective-permute-start.5 = (f32[2,1,1024,128]{3,2,1,0:T(8,128)}, f32[2,1,1024,128]{3,2,1,0:T(8,128)}, u32[]{:S(2)}, u32[]{:S(2)}) collective-permute-start(f32[2,1,1024,128]{3,2,1,0:T(8,128)} %get-tuple-element.421), channel_id=1, source_target_pairs={{16,0},{24,8},{32,16},{40,24},{48,32},{56,40},{64,48},{72,56},{80,... | collective-permute-start | bytes 3145736 | tf_op jit(solution)/shard_map/ppermute | solution.py:22
  441.5 88.0 %collective-permute-start.7 = (f32[2,1,1024,128]{3,2,1,0:T(8,128)}, f32[2,1,1024,128]{3,2,1,0:T(8,128)}, u32[]{:S(2)}, u32[]{:S(2)}) collective-permute-start(f32[2,1,1024,128]{3,2,1,0:T(8,128)} %get-tuple-element.422), channel_id=1, source_target_pairs={{32,0},{40,8},{48,16},{56,24},{64,32},{72,40},{80,48},{88,56},{96,... | collective-permute-start | bytes 3145736 | tf_op jit(solution)/shard_map/ppermute | solution.py:22
  444.2 103.1 %collective-permute-start.6 = (f32[2,1,1024,128]{3,2,1,0:T(8,128)S(1)}, f32[2,1,1024,128]{3,2,1,0:T(8,128)}, u32[]{:S(2)}, u32[]{:S(2)}) collective-permute-start(f32[2,1,1024,128]{3,2,1,0:T(8,128)S(1)} %get-tuple-element.423), channel_id=1, source_target_pairs={{24,0},{32,8},{40,16},{48,24},{56,32},{64,40},{72,48},{80,56},{88,... | collective-permute-start | bytes 3145736 | tf_op jit(solution)/shard_map/ppermute | solution.py:22
  446.2 110.9 %all-to-all-start.1 = ((bf16[8,128,384]{2,1,0:T(8,128)(2,1)}), bf16[8,128,384]{2,1,0:T(8,128)(2,1)S(1)}, u32[]{:S(2)}, u32[]{:S(2)}) async-start(bf16[8,128,384]{2,1,0:T(8,128)(2,1)} %bitcast.21), calls=%async_computation.1 | async-start | bytes 1572864 | tf_op jit(solution)/shard_map/all_to_all | solution.py:153
  547.4 15.8 %copy-start.16 = (bf16[3,1024,128]{2,1,0:T(8,128)(2,1)S(1)}, bf16[3,1024,128]{2,1,0:T(8,128)(2,1)}, u32[]{:S(2)}) copy-start(bf16[3,1024,128]{2,1,0:T(8,128)(2,1)} %param.17) | copy-start | bytes 2359300
  557.0 18.0 %all-to-all-start.2 = ((bf16[8,128,128]{2,1,0:T(8,128)(2,1)}), bf16[8,128,128]{2,1,0:T(8,128)(2,1)S(1)}, u32[]{:S(2)}, u32[]{:S(2)}) async-start(bf16[8,128,128]{2,1,0:T(8,128)(2,1)} %bitcast.26), calls=%async_computation.2 | async-start | bytes 524288 | tf_op jit(solution)/shard_map/all_to_all | solution.py:154
  575.0 129.8 %all-to-all-start.3 = ((bf16[8,128,128]{2,1,0:T(8,128)(2,1)}), bf16[8,128,128]{2,1,0:T(8,128)(2,1)S(1)}, u32[]{:S(2)}, u32[]{:S(2)}) async-start(bf16[8,128,128]{2,1,0:T(8,128)(2,1)} %bitcast.29), calls=%async_computation.3 | async-start | bytes 524288 | tf_op jit(solution)/shard_map/all_to_all | solution.py:155
  (29 other events, 128.0 us)
Sparse Core Ops, SparseCore 0:
  126.1 167.9 all-gather.1
